TPU v7x, 32 devices: a whole 2x2x4 slice. The times are simulated.
32 devices in a mesh: row: 4 (over z), col: 8 (over y, x, core).
Axes of the slice: x: 2, y: 2, z: 4, core: 2. Of those that a mesh axis runs over, the one named last changes fastest.
Arguments:
- inputs: bfloat16 [512, 8192], P(None, 'row'), may hold values from -6 to 6
- up_weight: bfloat16 [8192, 28672], P('row', 'col'), may hold values from -0.109375 to 0.109375
- down_weight: bfloat16 [28672, 8192], P('col', 'row'), may hold values from -0.0546875 to 0.0546875
- up_mask: int32 [64, 224], P('row', 'col'), may hold values 0 or 1
- down_mask: int32 [224, 64], P('col', 'row'), may hold values 0 or 1
- cotangent: bfloat16 [512, 8192], P(None, 'row'), may hold values from -6 to 6
Outputs:
- output: bfloat16 [512, 8192], P(None, 'row')
- input_grad: bfloat16 [512, 8192], P(None, 'row')
- up_grad: bfloat16 [8192, 28672], P('row', 'col')
- down_grad: bfloat16 [28672, 8192], P('col', 'row')
All inputs are finite; a program needn't handle non-finite values. No bound on the sum of `up_mask` or of `down_mask` on one device may be relied on, other than what follows from the above.
Results may differ from a plain program's by a relative error of at most 0.0051.
Values may be sent and summed in bfloat16 or wider, within the bound.
A program may use at most 128 MiB of HBM per device.

v0:
```python
import jax
import jax.numpy as jnp
from jax import lax
from jax.sharding import PartitionSpec as P


def expand(mask, block):
    kept = mask > 0
    return jnp.repeat(jnp.repeat(kept, block, axis=0), block, axis=1)


def activate(value):
    return jax.nn.gelu(value, approximate=True)


def body(inputs, up_weight, down_weight, up_mask, down_mask, cotangent):
    block = up_weight.shape[0] // up_mask.shape[0]
    keep_up = expand(up_mask, block)
    keep_down = expand(down_mask, block)
    masked_up = jnp.where(keep_up, up_weight, jnp.zeros_like(up_weight))
    masked_down = jnp.where(keep_down, down_weight, jnp.zeros_like(down_weight))
    hidden_part = jnp.dot(inputs, masked_up, preferred_element_type=jnp.float32)
    hidden_rows = lax.psum_scatter(hidden_part, "row", scatter_dimension=0, tiled=True)
    active_rows, pull_back = jax.vjp(activate, hidden_rows)
    active = lax.all_gather(active_rows.astype(jnp.bfloat16), "row", axis=0, tiled=True)
    output_part = jnp.dot(active, masked_down, preferred_element_type=jnp.float32)
    output = lax.psum(output_part, "col").astype(jnp.bfloat16)
    grad_part = jnp.dot(cotangent, masked_down.T, preferred_element_type=jnp.float32)
    grad_rows = lax.psum_scatter(grad_part, "row", scatter_dimension=0, tiled=True)
    local_grad = pull_back(grad_rows)[0].astype(jnp.bfloat16)
    hidden_grad = lax.all_gather(local_grad, "row", axis=0, tiled=True)
    input_part = jnp.dot(hidden_grad, masked_up.T, preferred_element_type=jnp.float32)
    input_grad = lax.psum(input_part, "col").astype(jnp.bfloat16)
    up_full = jnp.dot(inputs.T, hidden_grad, preferred_element_type=jnp.float32)
    up_grad = jnp.where(keep_up, up_full, jnp.zeros_like(up_full)).astype(jnp.bfloat16)
    down_full = jnp.dot(active.T, cotangent, preferred_element_type=jnp.float32)
    down_grad = jnp.where(keep_down, down_full, jnp.zeros_like(down_full)).astype(jnp.bfloat16)
    return (output, input_grad, up_grad, down_grad)


def solution(mesh):
    in_specs = (
        P(None, "row"),
        P("row", "col"),
        P("col", "row"),
        P("row", "col"),
        P("col", "row"),
        P(None, "row"),
    )
    out_specs = (P(None, "row"), P(None, "row"), P("row", "col"), P("col", "row"))
    return jax.shard_map(body, mesh=mesh, in_specs=in_specs, out_specs=out_specs, check_vma=False)
```

profile of v0, /device:TPU:0, one launch (start us, length us, event | category | flops | bytes accessed | tf_op | source)
XLA Modules:
  0.0 696.9 jit_solution(11580871956256539440)
XLA Ops:
  7.2 20.4 %copy.11 = bf16[2048,3584]{0,1:T(8,128)(2,1)} copy(bf16[2048,3584]{1,0:T(8,128)(2,1)} %param.7) | data formatting | bytes 29360128 | tf_op args[1]
  27.7 0.1 broadcast_bitcast_fusion
  27.9 7.4 %bitcast_select_fusion.1 = bf16[2048,3584]{0,1:T(8,128)(2,1)S(1)} fusion(bf16[2048,3584]{0,1:T(8,128)(2,1)} %copy.11, pred[2048,28]{0,1:T(8,128)(4,1)S(1)} %bitcast.40), kind=kLoop, calls=%fused_computation.1 | loop fusion | flops 7340032 | bytes 29417472 | tf_op jit(solution)/shard_map/jit(_where)/select_n | solution.py:20
  35.3 5.5 copy-done.1
  40.8 9.9 %convolution_bitcast_fusion = f32[512,3584]{0,1:T(8,128)} fusion(bf16[2048,3584]{0,1:T(8,128)(2,1)S(1)} %bitcast_select_fusion.1, bf16[512,2048]{1,0:T(8,128)(2,1)S(1)} %copy-done), kind=kOutput, calls=%fused_computation.9 | convolution fusion | flops 7516192768 | bytes 24117248 | tf_op jit(solution)/shard_map/dot_general | solution.py:22
  50.8 0.6 copy-done.4
  51.4 0.1 copy.12
  51.5 0.1 broadcast_in_dim.27
  51.7 23.3 %broadcast_in_dim.28 = pred[3584,16,128]{2,1,0:T(8,128)(4,1)S(1)} broadcast(pred[3584,16]{1,0:T(8,128)(4,1)S(1)} %bitcast.39), dimensions={0,1} | broadcast | bytes 7397376 | tf_op jit(solution)/shard_map/broadcast_in_dim | solution.py:9
  75.0 2.9 copy-done.2
  77.9 13.0 %fusion.5 = f32[512,3584]{0,1:T(8,128)} fusion(bf16[512,2048]{1,0:T(8,128)(2,1)S(1)} %copy-done.6, bf16[3584,2048]{1,0:T(8,128)(2,1)} %param.8, pred[448,8,16,128]{3,2,1,0:T(8,128)(4,1)S(1)} %bitcast.36), kind=kOutput, calls=%fused_computation.10 | convolution fusion | flops 7523532800 | bytes 31457280 | tf_op jit(solution)/shard_map/dot_general | solution.py:28
  91.0 90.3 %reduce-scatter.3.cloned.1.call-done = f32[128,3584]{0,1:T(8,128)} async-done(((f32[512,3584]{0,1:T(8,128)}), f32[128,3584]{0,1:T(8,128)}) %reduce-scatter.3.cloned.1.call-update) | async-done | bytes 1835024 | tf_op jit(solution)/shard_map/reduce_scatter | solution.py:23
  181.3 130.6 %reduce-scatter.5.cloned.1.call-done = f32[128,3584]{0,1:T(8,128)} async-done(((f32[512,3584]{0,1:T(8,128)}), f32[128,3584]{0,1:T(8,128)}) %reduce-scatter.5.cloned.1.call-update) | async-done | bytes 1835024 | tf_op jit(solution)/shard_map/reduce_scatter | solution.py:29
  311.9 4.6 fusion.12
  316.6 0.2 all-gather.5.cloned.1.call-start
  316.8 0.3 all-gather.5.cloned.1.call-update
  317.2 72.1 %all-gather.3.cloned.1.call-done = bf16[512,3584]{0,1:T(8,128)(2,1)} async-done(((bf16[128,3584]{0,1:T(8,128)(2,1)}), bf16[512,3584]{0,1:T(8,128)(2,1)}) %all-gather.3.cloned.1.call-update) | async-done | bytes 3670032 | tf_op jit(solution)/shard_map/all_gather | solution.py:25
  389.3 14.6 %fusion.2 = f32[512,2048]{1,0:T(8,128)} fusion(bf16[512,3584]{0,1:T(8,128)(2,1)} %all-gather.3.cloned.1.call-done, bf16[3584,2048]{1,0:T(8,128)(2,1)} %param.8, pred[448,8,16,128]{3,2,1,0:T(8,128)(4,1)} %bitcast.37), kind=kOutput, calls=%fused_computation.6 | convolution fusion | flops 7523532800 | bytes 29884416 | tf_op jit(solution)/shard_map/dot_general | solution.py:26
  403.9 57.6 %all-gather.5.cloned.1.call-done = bf16[512,3584]{0,1:T(8,128)(2,1)} async-done(((bf16[128,3584]{0,1:T(8,128)(2,1)}), bf16[512,3584]{0,1:T(8,128)(2,1)}) %all-gather.5.cloned.1.call-update) | async-done | bytes 3670032 | tf_op jit(solution)/shard_map/all_gather | solution.py:31
  461.5 15.6 %fusion.15 = f32[512,2048]{1,0:T(8,128)} fusion(bf16[512,3584]{0,1:T(8,128)(2,1)} %all-gather.5.cloned.1.call-done, bf16[2048,3584]{0,1:T(8,128)(2,1)} %copy-done.1), kind=kOutput, calls=%fused_computation.26 | convolution fusion | flops 7516192768 | bytes 22544384 | tf_op jit(solution)/shard_map/dot_general | solution.py:32
  477.1 11.0 %fusion = bf16[2048,3584]{0,1:T(8,128)(2,1)} fusion(bf16[512,3584]{0,1:T(8,128)(2,1)S(1)} %copy-done.5, bf16[512,2048]{1,0:T(8,128)(2,1)S(1)} %copy-done, pred[2048,28]{0,1:T(8,128)(4,1)S(1)} %bitcast.41), kind=kOutput, calls=%fused_computation.2 | convolution fusion | flops 7530872832 | bytes 20504576 | tf_op jit(solution)/shard_map/dot_general | solution.py:34
  488.1 18.6 %copy.13 = bf16[2048,3584]{1,0:T(8,128)(2,1)} copy(bf16[2048,3584]{0,1:T(8,128)(2,1)} %fusion) | data formatting | bytes 29360128
  506.7 169.0 %all-reduce.2 = (bf16[512,2048]{1,0:T(8,128)(2,1)}, bf16[512,2048]{1,0:T(8,128)(2,1)}) all-reduce(f32[512,2048]{1,0:T(8,128)} %fusion.2, f32[512,2048]{1,0:T(8,128)} %fusion.15), channel_id=1, replica_groups=mesh['row'=4,'col'=8] {'col'}, use_global_device_ids=true, to_apply=%region_1.2 | all-reduce | flops 2097152 | bytes 12582912 | tf_op jit(solution)/shard_map/psum | solution.py:27
  675.7 14.7 %select_convert_fusion = bf16[3584,2048]{1,0:T(8,128)(2,1)} fusion(pred[448,8,16,128]{3,2,1,0:T(8,128)(4,1)} %bitcast.38, bf16[512,3584]{0,1:T(8,128)(2,1)} %all-gather.3.cloned.1.call-done, bf16[512,2048]{1,0:T(8,128)(2,1)} %param.11), kind=kOutput, calls=%fused_computation.3 | convolution fusion | flops 7530872832 | bytes 27787264 | tf_op jit(solution)/shard_map/dot_general | solution.py:36
  (22 shorter events, 0.4 us)
Async XLA Ops:
  7.2 33.6 %copy-start = (bf16[512,2048]{1,0:T(8,128)(2,1)S(1)}, bf16[512,2048]{1,0:T(8,128)(2,1)}, u32[]{:S(2)}) copy-start(bf16[512,2048]{1,0:T(8,128)(2,1)} %param.6) | copy-start | bytes 6291460
  7.2 20.4 %copy-start.3 = (s32[16,28]{1,0:T(8,128)S(1)}, s32[16,28]{1,0:T(8,128)}, u32[]{:S(2)}) copy-start(s32[16,28]{1,0:T(8,128)} %param.9) | copy-start | bytes 5380
  7.2 174.2 %reduce-scatter.3.cloned.1.call-start = ((), (), s32[]{:S(2)}) async-start(), calls=%async_computation.2 | async-start | bytes 9175040 | tf_op jit(solution)/shard_map/reduce_scatter | solution.py:23
  35.3 5.5 copy-start.1
  50.7 0.7 copy-start.4
  50.7 261.2 %reduce-scatter.5.cloned.1.call-start = ((), (), s32[]{:S(2)}) async-start(), calls=%async_computation.4 | async-start | bytes 9175040 | tf_op jit(solution)/shard_map/reduce_scatter | solution.py:29
  51.6 26.3 %copy-start.6 = (bf16[512,2048]{1,0:T(8,128)(2,1)S(1)}, bf16[512,2048]{1,0:T(8,128)(2,1)}, u32[]{:S(2)}) copy-start(bf16[512,2048]{1,0:T(8,128)(2,1)} %param.11) | copy-start | bytes 6291460
  75.0 2.9 copy-start.2
  91.0 298.3 %all-gather.3.cloned.1.call-start = ((), (), s32[]{:S(2)}) async-start(), calls=%async_computation.3 | async-start | bytes 4587520 | tf_op jit(solution)/shard_map/all_gather | solution.py:25
  316.6 144.9 %all-gather.5.cloned.1.call-start = ((), (), s32[]{:S(2)}) async-start(), calls=%async_computation.5 | async-start | bytes 4587520 | tf_op jit(solution)/shard_map/all_gather | solution.py:31
  461.5 15.6 %copy-start.5 = (bf16[512,3584]{0,1:T(8,128)(2,1)S(1)}, bf16[512,3584]{0,1:T(8,128)(2,1)}, u32[]{:S(2)}) copy-start(bf16[512,3584]{0,1:T(8,128)(2,1)} %all-gather.5.cloned.1.call-done) | copy-start | bytes 11010052
Sparse Core Ops, SparseCore 0:
  50.9 130.4 reduce-scatter.2
  183.6 128.2 reduce-scatter.4
  316.7 72.4 all-gather.2
  391.3 70.1 all-gather.4
where the time goes:
time: 698 us; the launch traced here: 697 us
  waiting for transfers between devices  351 us (50%)
  blocking collectives  169 us (24%)
  matrix products  78.9 us (11%)
  local copies, waits for them, and re-layouts  71.9 us (10%)
  between operations  13.9 us (2%)
  other arithmetic  12.1 us (2%)
    psum x1, blocking collectives, body(): output = lax.psum(output_part, 'col').astype(jnp.bfloat16)  169 us
    reduce_scatter x1, waiting for transfers between devices, body(): lax.psum_scatter(grad_part, 'row', scatter_dimension=0, tiled=True)  131 us
    reduce_scatter x1, waiting for transfers between devices, body(): lax.psum_scatter(hidden_part, 'row', scatter_dimension=0, tiled=True)  90.3 us
    all_gather x1, waiting for transfers between devices, body(): lax.all_gather(active_rows.astype(jnp.bfloat16), 'row', axis=0, tiled=True)  72.1 us
    all_gather x1, waiting for transfers between devices, body(): hidden_grad = lax.all_gather(local_grad, 'row', axis=0, tiled=True)  57.6 us
    unnamed x19, local copies, waits for them, and re-layouts  48.2 us
    broadcast_in_dim x2, local copies, waits for them, and re-layouts, expand(): return jnp.repeat(jnp.repeat(kept, block, axis=0), block, axis=1)  23.4 us
    dot_general x1, matrix products, body(): jnp.dot(hidden_grad, masked_up.T, preferred_element_type=jnp.float32)  15.6 us
  transfers between devices with their start and end apart: 4, of which 4 were waited for; matrix products, arithmetic and copies ran while one was open for 7% of the time, Pallas kernels for 0%

commit v1 on v0

v1 whole, which is shorter than its diff:
```python
import functools

import jax
import jax.numpy as jnp
from jax import lax
from jax.experimental import pallas as pl
from jax.experimental.pallas import tpu as pltpu
from jax.sharding import PartitionSpec as P

MESH = pl.DeviceIdType.MESH
F32 = jnp.float32
BF16 = jnp.bfloat16
SLOTS = 6
DEFER = 2
LIMIT = 63 * 1024 * 1024
NT = (((1,), (1,)), ((), ()))
TN = (((0,), (0,)), ((), ()))
ROOT = 0.7978845608028654
CUBE = 0.044715


def gelu_and_slope(v):
    square = v * v
    tanh = jnp.tanh(ROOT * v * (1.0 + CUBE * square))
    half = 0.5 * (1.0 + tanh)
    slope = half + 0.5 * v * (1.0 - tanh * tanh) * (ROOT * (1.0 + 3.0 * CUBE * square))
    return v * half, slope


def layer_kernel(
    rows, cols, halves, width, block,
    x, ct, up_hbm, dn_hbm, keep_up, keep_dn,
    sums, act_hbm, hg_hbm,
    up_v, dn_v, acc, to_inner, from_outer, from_inner,
    pair_out, pair_in, half, chip_in, fin,
    w_sem, in_send, out_recv, in_recv, out_send, store_sem, cred_in, cred_out,
    s0, r0, s1, r1, s2, r2, s3, r3, own_sem,
):
    tokens, d_model = x.shape
    chunks = up_v.shape[0]
    tm = tokens // halves
    steps = halves * chunks
    chips = cols // 2
    part = tm // cols
    me_r, me_c = lax.axis_index("row"), lax.axis_index("col")
    chip, core = lax.div(me_c, 2), lax.rem(me_c, 2)
    sibling = (me_r, chip * 2 + 1 - core)
    mid = rows // 2
    left = me_r < mid
    toward = jnp.where(left, 1, -1)
    dist = jnp.where(left, mid - 1 - me_r, me_r - mid)
    is_mid = dist == 0
    has_outer = jnp.logical_and(me_r > 0, me_r < rows - 1)
    inner = (me_r + toward, me_c)
    outer = (lax.rem(me_r - toward + rows, rows), me_c)
    lag = 2 + 3 * dist

    def chip_peer(j):
        return (me_r, lax.rem(chip + j, chips) * 2 + core)

    def weight_copies(c):
        at = pl.multiple_of(c * width, width)
        return (
            pltpu.make_async_copy(up_hbm.at[:, pl.ds(at, width)], up_v.at[c], w_sem.at[0, c]),
            pltpu.make_async_copy(dn_hbm.at[pl.ds(at, width), :], dn_v.at[c], w_sem.at[1, c]),
        )

    @pl.loop(0, chunks)
    def _(c):
        for copy in weight_copies(c):
            copy.start()

    barrier = pltpu.get_barrier_semaphore()
    greet = [inner, sibling] + [chip_peer(j) for j in range(1, chips)]
    for device in greet:
        pl.semaphore_signal(barrier, inc=1, device_id=device, device_id_type=MESH)

    @pl.when(has_outer)
    def _():
        pl.semaphore_signal(barrier, inc=1, device_id=outer, device_id_type=MESH)

    for t in range(halves):
        for which in range(2):
            acc[t, which] = jnp.zeros((tm, d_model), F32)

    @pl.when(has_outer)
    def _():
        pl.semaphore_wait(barrier, len(greet) + 1)

    @pl.when(jnp.logical_not(has_outer))
    def _():
        pl.semaphore_wait(barrier, len(greet))

    def inward(k, middle):
        return pltpu.make_async_remote_copy(
            src_ref=to_inner.at[k],
            dst_ref=from_inner.at[k] if middle else from_outer.at[k],
            send_sem=in_send.at[k],
            recv_sem=in_recv.at[k] if middle else out_recv.at[k],
            device_id=inner,
            device_id_type=MESH,
        )

    def outward(k):
        return pltpu.make_async_remote_copy(
            src_ref=from_inner.at[k],
            dst_ref=from_inner.at[k],
            send_sem=out_send.at[k],
            recv_sem=in_recv.at[k],
            device_id=outer,
            device_id_type=MESH,
        )

    def stores(u):
        k = lax.rem(u, SLOTS)
        row = pl.multiple_of(lax.div(u, chunks) * tm, tm)
        col = pl.multiple_of(lax.rem(u, chunks) * width, width)
        there = (pl.ds(row, tm), pl.ds(col, width))
        return (
            pltpu.make_async_copy(from_inner.at[k, 0], act_hbm.at[there], store_sem.at[0, k]),
            pltpu.make_async_copy(from_inner.at[k, 1], hg_hbm.at[there], store_sem.at[1, k]),
        )

    def apply_mask(c):
        per = width // block

        @pl.loop(0, d_model // block)
        def _(b):
            at = pl.ds(pl.multiple_of(b * block, block), block)
            for j in range(per):
                lanes = pl.ds(j * block, block)
                keep = keep_up[b, c * per + j]
                up_v[c, at, lanes] = (up_v[c, at, lanes].astype(F32) * keep).astype(BF16)
                keep = keep_dn[c * per + j, b]
                dn_v[c, lanes, at] = (dn_v[c, lanes, at].astype(F32) * keep).astype(BF16)

    def produce(s):
        t, c, k = lax.div(s, chunks), lax.rem(s, chunks), lax.rem(s, SLOTS)

        @pl.when(t == 0)
        def _():
            for copy in weight_copies(c):
                copy.wait()
            apply_mask(c)

        token = pl.ds(pl.multiple_of(t * tm, tm), tm)
        h = jnp.dot(x[token, :], up_v[c], preferred_element_type=F32)
        g = lax.dot_general(ct[token, :], dn_v[c], NT, preferred_element_type=F32)

        @pl.when(s >= SLOTS)
        def _():
            inward(k, True).wait_send()
            pl.semaphore_wait(cred_in, 1)

        @pl.when(has_outer)
        def _():
            outward_in(k).wait_recv()
            to_inner[k, 0] = (h + from_outer[k, 0].astype(F32)).astype(BF16)
            to_inner[k, 1] = (g + from_outer[k, 1].astype(F32)).astype(BF16)

            @pl.when(s + SLOTS < steps)
            def _():
                pl.semaphore_signal(cred_in, inc=1, device_id=outer, device_id_type=MESH)

        @pl.when(jnp.logical_not(has_outer))
        def _():
            to_inner[k, 0] = h.astype(BF16)
            to_inner[k, 1] = g.astype(BF16)

        @pl.when(is_mid)
        def _():
            inward(k, True).start()

        @pl.when(jnp.logical_not(is_mid))
        def _():
            inward(k, False).start()

    def outward_in(k):
        return inward(k, False)

    def release(u):
        k = lax.rem(u, SLOTS)
        for copy in stores(u):
            copy.wait()

        @pl.when(has_outer)
        def _():
            outward(k).wait_send()

        @pl.when(u + SLOTS < steps)
        def _():
            @pl.when(is_mid)
            def _():
                pl.semaphore_signal(cred_in, inc=1, device_id=inner, device_id_type=MESH)

            @pl.when(jnp.logical_not(is_mid))
            def _():
                pl.semaphore_signal(cred_out, inc=1, device_id=inner, device_id_type=MESH)

    def consume(u):
        t, c, k = lax.div(u, chunks), lax.rem(u, chunks), lax.rem(u, SLOTS)
        outward(k).wait_recv()

        @pl.when(is_mid)
        def _():
            h = to_inner[k, 0].astype(F32) + from_inner[k, 0].astype(F32)
            g = to_inner[k, 1].astype(F32) + from_inner[k, 1].astype(F32)
            active, slope = gelu_and_slope(h)
            from_inner[k, 0] = active.astype(BF16)
            from_inner[k, 1] = (g * slope).astype(BF16)

        @pl.when(has_outer)
        def _():
            @pl.when(u >= SLOTS)
            def _():
                pl.semaphore_wait(cred_out, 1)

            outward(k).start()

        for copy in stores(u):
            copy.start()
        acc[t, 0] += jnp.dot(from_inner[k, 0], dn_v[c], preferred_element_type=F32)
        acc[t, 1] += lax.dot_general(from_inner[k, 1], up_v[c], NT, preferred_element_type=F32)

        @pl.when(u >= DEFER)
        def _():
            release(u - DEFER)

    def rows_of(t, owner, first, count):
        return pl.ds(pl.multiple_of(t * tm + owner * (tm // 2) + first, part), count)

    def pair_copy(t):
        return pltpu.make_async_remote_copy(
            src_ref=pair_out.at[t], dst_ref=pair_in.at[t], send_sem=s0.at[t], recv_sem=r0.at[t],
            device_id=sibling, device_id_type=MESH)

    def chip_copy(t, j):
        return pltpu.make_async_remote_copy(
            src_ref=half.at[t, lax.rem(chip + j, chips)], dst_ref=chip_in.at[t, j - 1],
            send_sem=s1.at[t, j - 1], recv_sem=r1.at[t, j - 1],
            device_id=chip_peer(j), device_id_type=MESH)

    def spread_copy(t, j):
        mine = rows_of(t, core, chip * part, part)
        return pltpu.make_async_remote_copy(
            src_ref=fin.at[t], dst_ref=sums.at[:, mine, :],
            send_sem=s2.at[t, j - 1], recv_sem=r2.at[t, j - 1],
            device_id=chip_peer(j), device_id_type=MESH)

    def own_copy(t):
        mine = rows_of(t, core, chip * part, part)
        return pltpu.make_async_copy(fin.at[t], sums.at[:, mine, :], own_sem.at[t])

    def share_copy(t):
        mine = rows_of(t, core, 0, tm // 2)
        return pltpu.make_async_remote_copy(
            src_ref=sums.at[:, mine, :], dst_ref=sums.at[:, mine, :], send_sem=s3.at[t], recv_sem=r3.at[t],
            device_id=sibling, device_id_type=MESH)

    def phase0(t):
        other = pl.ds(pl.multiple_of((1 - core) * (tm // 2), tm // 2), tm // 2)
        for which in range(2):
            pair_out[t, which] = acc[t, which, other, :].astype(BF16)
        pair_copy(t).start()

    def phase1(t):
        pair_copy(t).wait()

        @pl.loop(0, chips)
        def _(q):
            mine = pl.ds(pl.multiple_of(core * (tm // 2) + q * part, part), part)
            there = pl.ds(pl.multiple_of(q * part, part), part)
            for which in range(2):
                half[t, q, which] = (acc[t, which, mine, :] + pair_in[t, which, there, :].astype(F32)).astype(BF16)

        for j in range(1, chips):
            chip_copy(t, j).start()

    def phase2(t):
        for j in range(1, chips):
            chip_copy(t, j).wait()
        for which in range(2):
            total = half[t, chip, which].astype(F32)
            for j in range(1, chips):
                total = total + chip_in[t, j - 1, which].astype(F32)
            fin[t, which] = total.astype(BF16)
        own_copy(t).start()
        for j in range(1, chips):
            spread_copy(t, j).start()

    def phase3(t):
        own_copy(t).wait()
        for j in range(1, chips):
            spread_copy(t, j).wait()
        share_copy(t).start()

    def phase4(t):
        share_copy(t).wait()

    phases = ((0, phase0), (2, phase1), (4, phase2), (6, phase3))
    late = []

    @pl.loop(0, steps + lag)
    def _(s):
        @pl.when(s < steps)
        def _():
            produce(s)

        @pl.when(s >= lag)
        def _():
            u = s - lag
            consume(u)
            for t in range(halves):
                for after, phase in phases:
                    at = (t + 1) * chunks - 1 + after
                    if at < steps:
                        @pl.when(u == at)
                        def _(phase=phase, t=t):
                            phase(t)

    for t in range(halves):
        for after, phase in phases:
            if (t + 1) * chunks - 1 + after >= steps:
                phase(t)
    for u in range(steps - DEFER, steps):
        release(u)

    @pl.loop(steps - SLOTS, steps)
    def _(s):
        inward(lax.rem(s, SLOTS), True).wait_send()

    for t in range(halves):
        phase4(t)


def grads_kernel(block, x, ct, act, hg, keep_up, keep_dn, up_out, dn_out, xt):
    c = pl.program_id(0)
    width = hg.shape[1]
    per = width // block

    @pl.when(c == 0)
    def _():
        xt[...] = x[...].T

    @pl.loop(0, xt.shape[0] // block // 2)
    def _(pair):
        at = pl.ds(pl.multiple_of(pair * 2 * block, 2 * block), 2 * block)
        full = jnp.dot(xt[at, :], hg[...], preferred_element_type=F32)
        for i in range(2):
            for j in range(per):
                lanes = slice(j * block, (j + 1) * block)
                keep = keep_up[pair * 2 + i, c * per + j]
                there = pl.ds(pl.multiple_of((pair * 2 + i) * block, block), block)
                up_out[there, lanes] = (full[i * block:(i + 1) * block, lanes] * keep).astype(BF16)

    at_t = act[...].T

    @pl.loop(0, ct.shape[1] // block // 2)
    def _(pair):
        at = pl.ds(pl.multiple_of(pair * 2 * block, 2 * block), 2 * block)
        full = jnp.dot(at_t, ct[:, at], preferred_element_type=F32)
        for i in range(2):
            there = pl.ds(pl.multiple_of((pair * 2 + i) * block, block), block)
            for j in range(per):
                lanes = slice(j * block, (j + 1) * block)
                keep = keep_dn[c * per + j, pair * 2 + i]
                dn_out[lanes, there] = (full[lanes, i * block:(i + 1) * block] * keep).astype(BF16)


def body(rows, cols, inputs, up_weight, down_weight, up_mask, down_mask, cotangent):
    tokens, d_model = inputs.shape
    hidden = up_weight.shape[1]
    block = d_model // up_mask.shape[0]
    keep_up = (up_mask > 0).astype(F32)
    keep_dn = (down_mask > 0).astype(F32)
    width = 2 * block if hidden % (2 * block) == 0 else block
    chunks = hidden // width
    halves = 2
    tm = tokens // halves
    chips = cols // 2
    part = tm // cols
    vmem = pl.BlockSpec(memory_space=pltpu.VMEM)
    smem = pl.BlockSpec(memory_space=pltpu.SMEM)
    hbm = pl.BlockSpec(memory_space=pl.ANY)
    dma = pltpu.SemaphoreType.DMA
    sums, act, hg = pl.pallas_call(
        functools.partial(layer_kernel, rows, cols, halves, width, block),
        out_shape=(
            jax.ShapeDtypeStruct((2, tokens, d_model), BF16),
            jax.ShapeDtypeStruct((tokens, hidden), BF16),
            jax.ShapeDtypeStruct((tokens, hidden), BF16),
        ),
        in_specs=[vmem, vmem, hbm, hbm, smem, smem],
        out_specs=(hbm, hbm, hbm),
        scratch_shapes=[
            pltpu.VMEM((chunks, d_model, width), BF16),
            pltpu.VMEM((chunks, width, d_model), BF16),
            pltpu.VMEM((halves, 2, tm, d_model), F32),
            pltpu.VMEM((SLOTS, 2, tm, width), BF16),
            pltpu.VMEM((SLOTS, 2, tm, width), BF16),
            pltpu.VMEM((SLOTS, 2, tm, width), BF16),
            pltpu.VMEM((halves, 2, tm // 2, d_model), BF16),
            pltpu.VMEM((halves, 2, tm // 2, d_model), BF16),
            pltpu.VMEM((halves, chips, 2, part, d_model), BF16),
            pltpu.VMEM((halves, max(chips - 1, 1), 2, part, d_model), BF16),
            pltpu.VMEM((halves, 2, part, d_model), BF16),
            dma((2, chunks)),
            dma((SLOTS,)), dma((SLOTS,)), dma((SLOTS,)), dma((SLOTS,)),
            dma((2, SLOTS)),
            pltpu.SemaphoreType.REGULAR, pltpu.SemaphoreType.REGULAR,
            dma((halves,)), dma((halves,)),
            dma((halves, max(chips - 1, 1))), dma((halves, max(chips - 1, 1))),
            dma((halves, max(chips - 1, 1))), dma((halves, max(chips - 1, 1))),
            dma((halves,)), dma((halves,)),
            dma((halves,)),
        ],
        compiler_params=pltpu.CompilerParams(collective_id=0, has_side_effects=True, vmem_limit_bytes=LIMIT),
        cost_estimate=pl.CostEstimate(
            flops=8 * tokens * d_model * hidden, bytes_accessed=4 * d_model * hidden, transcendentals=tokens * hidden),
    )(inputs, cotangent, up_weight, down_weight, keep_up, keep_dn)

    wide = next(w for w in (4 * block, 2 * block, block) if hidden % w == 0)
    up_grad, down_grad = pl.pallas_call(
        functools.partial(grads_kernel, block),
        grid=(hidden // wide,),
        out_shape=(
            jax.ShapeDtypeStruct((d_model, hidden), BF16),
            jax.ShapeDtypeStruct((hidden, d_model), BF16),
        ),
        in_specs=[
            pl.BlockSpec((tokens, d_model), lambda c: (0, 0)),
            pl.BlockSpec((tokens, d_model), lambda c: (0, 0)),
            pl.BlockSpec((tokens, wide), lambda c: (0, c)),
            pl.BlockSpec((tokens, wide), lambda c: (0, c)),
            smem, smem,
        ],
        out_specs=(
            pl.BlockSpec((d_model, wide), lambda c: (0, c)),
            pl.BlockSpec((wide, d_model), lambda c: (c, 0)),
        ),
        scratch_shapes=[pltpu.VMEM((d_model, tokens), BF16)],
        compiler_params=pltpu.CompilerParams(vmem_limit_bytes=48 * 1024 * 1024),
        cost_estimate=pl.CostEstimate(
            flops=4 * tokens * d_model * hidden, bytes_accessed=4 * d_model * hidden, transcendentals=0),
    )(inputs, cotangent, act, hg, keep_up, keep_dn)
    return (sums[0], sums[1], up_grad, down_grad)


def solution(mesh):
    in_specs = (
        P(None, "row"),
        P("row", "col"),
        P("col", "row"),
        P("row", "col"),
        P("col", "row"),
        P(None, "row"),
    )
    out_specs = (P(None, "row"), P(None, "row"), P("row", "col"), P("col", "row"))
    step = functools.partial(body, mesh.shape["row"], mesh.shape["col"])
    return jax.shard_map(step, mesh=mesh, in_specs=in_specs, out_specs=out_specs, check_vma=False)
```

time: 698 us -> 269 us (0.39)
  waiting for transfers between devices: 351 us -> 0 us
  Pallas kernels: 0 us -> 260 us
  blocking collectives: 169 us -> 0 us
  matrix products: 78.9 us -> 0 us
  local copies, waits for them, and re-layouts: 71.9 us -> 5.78 us
  between operations: 13.9 us -> 0.68 us
  other arithmetic: 12.1 us -> 1.91 us
    pallas_call x0 -> x2, Pallas kernels: none -> 260 us  [the longest x1 218 us: body(): pl.pallas_call(functools.partial(layer_kernel, rows, cols, halves, width,...]
    reduce_scatter x2 -> x0, waiting for transfers between devices: 221 us -> none  [the longest x1 131 us: body(): lax.psum_scatter(grad_part, 'row', scatter_dimension=0, tiled=True)]
    psum x1 -> x0, blocking collectives: 169 us -> none  [body(): output = lax.psum(output_part, 'col').astype(jnp.bfloat16)]
    all_gather x2 -> x0, waiting for transfers between devices: 130 us -> none  [the longest x1 72.1 us: body(): lax.all_gather(active_rows.astype(jnp.bfloat16), 'row', axis=0, tiled=True)]
    dot_general x6 -> x0, matrix products: 78.9 us -> none  [the longest x1 15.6 us: body(): jnp.dot(hidden_grad, masked_up.T, preferred_element_type=jnp.float32)]
    unnamed x19 -> x9, local copies, waits for them, and re-layouts: 48.2 us -> 0.81 us
    broadcast_in_dim x2 -> x0, local copies, waits for them, and re-layouts: 23.4 us -> none  [expand(): return jnp.repeat(jnp.repeat(kept, block, axis=0), block, axis=1)]
    select_n x1 -> x0, other arithmetic: 7.4 us -> none  [body(): masked_up = jnp.where(keep_up, up_weight, jnp.zeros_like(up_weight))]
  transfers between devices with their start and end apart: 4 -> 0, of which waited for: 4 -> 0; matrix products, arithmetic and copies ran while one was open for 7% -> 0% of each run, Pallas kernels for 0% -> 0%
where the time goes in v1:
time: 269 us; the launch traced here: 268 us
  Pallas kernels  260 us (97%)
  local copies, waits for them, and re-layouts  5.78 us (2%)
    pallas_call x1, Pallas kernels, body(): pl.pallas_call(functools.partial(layer_kernel, rows, cols, halves, width,...  218 us
    pallas_call x1, Pallas kernels, body(): pl.pallas_call(functools.partial(grads_kernel, block), grid=(hidden // wi...  41.7 us

profile of v1, /device:TPU:0, one launch (start us, length us, event | category | flops | bytes accessed | tf_op | source)
XLA Modules:
  0.0 268.3 jit_solution(18061625684307387641)
XLA Ops:
  0.6 1.3 compare_convert_fusion.1.keep_up
  1.9 0.8 copy.10
  2.7 0.6 compare_convert_fusion.keep_dn
  3.3 218.2 %shard_map.93 = (bf16[2,512,2048]{2,1,0:T(8,128)(2,1)}, bf16[512,3584]{1,0:T(8,128)(2,1)}, bf16[512,3584]{1,0:T(8,128)(2,1)}) custom-call(bf16[512,2048]{1,0:T(8,128)(2,1)} %x.3, bf16[512,2048]{1,0:T(8,128)(2,1)} %ct.3, bf16[2048,3584]{1,0:T(8,128)(2,1)} %up_hbm.1, bf16[3584,2048]{1,0:T(8,128)(2,1)} %dn_hbm.1, f32[16,28]{1,0:T(8,128)} %compare_convert_fusion.1.keep_up, ...), custom_call_target="tpu_custom_call" | custom-call | flops 30064771072 | bytes 29360128 | tf_op jit(solution)/shard_map/pallas_call | solution.py:386
  221.5 0.0 copy-start
  221.6 0.0 copy-start.1
  221.6 0.0 copy-start.2
  221.6 0.0 copy-start.3
  221.6 5.0 %slice_bitcast_fusion = (bf16[512,2048]{1,0:T(8,128)(2,1)}, bf16[512,2048]{1,0:T(8,128)(2,1)}) fusion(bf16[2,512,2048]{2,1,0:T(8,128)(2,1)} %get-tuple-element.9), kind=kLoop, calls=%fused_computation | loop fusion | bytes 8388608 | tf_op jit(solution)/shard_map/squeeze | solution.py:446
  226.6 0.0 copy-done
  226.6 0.0 copy-done.1
  226.6 0.0 copy-done.2
  226.6 0.0 copy-done.3
  226.6 41.7 %shard_map.94 = (bf16[2048,3584]{1,0:T(8,128)(2,1)}, bf16[3584,2048]{1,0:T(8,128)(2,1)}) custom-call(bf16[512,2048]{1,0:T(8,128)(2,1)S(1)} %copy-done.2, bf16[512,2048]{1,0:T(8,128)(2,1)S(1)} %copy-done.3, bf16[512,3584]{1,0:T(8,128)(2,1)} %get-tuple-element.10.act, bf16[512,3584]{1,0:T(8,128)(2,1)} %get-tuple-element.11.hg, f32[16,28]{1,0:T(8,128)S(1)} %copy-done.1, ...), custom_call_target="tpu_custom_call" | custom-call | flops 15032385536 | bytes 29360128 | tf_op jit(solution)/shard_map/pallas_call | solution.py:423
Async XLA Ops:
  221.5 5.0 %copy-start = (f32[28,16]{1,0:T(8,128)S(1)}, f32[28,16]{1,0:T(8,128)}, u32[]{:S(2)}) copy-start(f32[28,16]{1,0:T(8,128)} %compare_convert_fusion.keep_dn) | copy-start | bytes 5380
  221.6 5.0 %copy-start.1 = (f32[16,28]{1,0:T(8,128)S(1)}, f32[16,28]{1,0:T(8,128)}, u32[]{:S(2)}) copy-start(f32[16,28]{1,0:T(8,128)} %compare_convert_fusion.1.keep_up) | copy-start | bytes 5380
  221.6 5.0 %copy-start.2 = (bf16[512,2048]{1,0:T(8,128)(2,1)S(1)}, bf16[512,2048]{1,0:T(8,128)(2,1)}, u32[]{:S(2)}) copy-start(bf16[512,2048]{1,0:T(8,128)(2,1)} %x.3) | copy-start | bytes 6291460
  221.6 5.0 %copy-start.3 = (bf16[512,2048]{1,0:T(8,128)(2,1)S(1)}, bf16[512,2048]{1,0:T(8,128)(2,1)}, u32[]{:S(2)}) copy-start(bf16[512,2048]{1,0:T(8,128)(2,1)} %ct.3) | copy-start | bytes 6291460

commit v2 on v1

--- a/solution.py
+++ b/solution.py
@@ -10,7 +10,6 @@
 MESH = pl.DeviceIdType.MESH
 F32 = jnp.float32
 BF16 = jnp.bfloat16
-SLOTS = 6
 DEFER = 2
 LIMIT = 63 * 1024 * 1024
 NT = (((1,), (1,)), ((), ()))
@@ -27,11 +26,16 @@
     return v * half, slope
 
 
+def splat(keep, block):
+    tile = jnp.full((16, block), keep.astype(F32)).astype(BF16)
+    return jnp.broadcast_to(tile[None], (block // 16, 16, block)).reshape(block, block)
+
+
 def layer_kernel(
-    rows, cols, halves, width, block,
+    rows, cols, halves, width, block, slots,
     x, ct, up_hbm, dn_hbm, keep_up, keep_dn,
     sums, act_hbm, hg_hbm,
-    up_v, dn_v, acc, to_inner, from_outer, from_inner,
+    up_v, dn_v, acc, to_inner, from_outer, from_inner, turned,
     pair_out, pair_in, half, chip_in, fin,
     w_sem, in_send, out_recv, in_recv, out_send, store_sem, cred_in, cred_out,
     s0, r0, s1, r1, s2, r2, s3, r3, own_sem,
@@ -112,13 +116,13 @@
         )
 
     def stores(u):
-        k = lax.rem(u, SLOTS)
+        k = lax.rem(u, slots)
         row = pl.multiple_of(lax.div(u, chunks) * tm, tm)
         col = pl.multiple_of(lax.rem(u, chunks) * width, width)
-        there = (pl.ds(row, tm), pl.ds(col, width))
+        token, unit = pl.ds(row, tm), pl.ds(col, width)
         return (
-            pltpu.make_async_copy(from_inner.at[k, 0], act_hbm.at[there], store_sem.at[0, k]),
-            pltpu.make_async_copy(from_inner.at[k, 1], hg_hbm.at[there], store_sem.at[1, k]),
+            pltpu.make_async_copy(turned.at[k], act_hbm.at[unit, token], store_sem.at[0, k]),
+            pltpu.make_async_copy(from_inner.at[k, 1], hg_hbm.at[token, unit], store_sem.at[1, k]),
         )
 
     def apply_mask(c):
@@ -129,13 +133,11 @@
             at = pl.ds(pl.multiple_of(b * block, block), block)
             for j in range(per):
                 lanes = pl.ds(j * block, block)
-                keep = keep_up[b, c * per + j]
-                up_v[c, at, lanes] = (up_v[c, at, lanes].astype(F32) * keep).astype(BF16)
-                keep = keep_dn[c * per + j, b]
-                dn_v[c, lanes, at] = (dn_v[c, lanes, at].astype(F32) * keep).astype(BF16)
+                up_v[c, at, lanes] = up_v[c, at, lanes] * splat(keep_up[b, c * per + j], block)
+                dn_v[c, lanes, at] = dn_v[c, lanes, at] * splat(keep_dn[c * per + j, b], block)
 
     def produce(s):
-        t, c, k = lax.div(s, chunks), lax.rem(s, chunks), lax.rem(s, SLOTS)
+        t, c, k = lax.div(s, chunks), lax.rem(s, chunks), lax.rem(s, slots)
 
         @pl.when(t == 0)
         def _():
@@ -147,7 +149,7 @@
         h = jnp.dot(x[token, :], up_v[c], preferred_element_type=F32)
         g = lax.dot_general(ct[token, :], dn_v[c], NT, preferred_element_type=F32)
 
-        @pl.when(s >= SLOTS)
+        @pl.when(s >= slots)
         def _():
             inward(k, True).wait_send()
             pl.semaphore_wait(cred_in, 1)
@@ -158,7 +160,7 @@
             to_inner[k, 0] = (h + from_outer[k, 0].astype(F32)).astype(BF16)
             to_inner[k, 1] = (g + from_outer[k, 1].astype(F32)).astype(BF16)
 
-            @pl.when(s + SLOTS < steps)
+            @pl.when(s + slots < steps)
             def _():
                 pl.semaphore_signal(cred_in, inc=1, device_id=outer, device_id_type=MESH)
 
@@ -179,7 +181,7 @@
         return inward(k, False)
 
     def release(u):
-        k = lax.rem(u, SLOTS)
+        k = lax.rem(u, slots)
         for copy in stores(u):
             copy.wait()
 
@@ -187,7 +189,7 @@
         def _():
             outward(k).wait_send()
 
-        @pl.when(u + SLOTS < steps)
+        @pl.when(u + slots < steps)
         def _():
             @pl.when(is_mid)
             def _():
@@ -198,7 +200,7 @@
                 pl.semaphore_signal(cred_out, inc=1, device_id=inner, device_id_type=MESH)
 
     def consume(u):
-        t, c, k = lax.div(u, chunks), lax.rem(u, chunks), lax.rem(u, SLOTS)
+        t, c, k = lax.div(u, chunks), lax.rem(u, chunks), lax.rem(u, slots)
         outward(k).wait_recv()
 
         @pl.when(is_mid)
@@ -211,12 +213,13 @@
 
         @pl.when(has_outer)
         def _():
-            @pl.when(u >= SLOTS)
+            @pl.when(u >= slots)
             def _():
                 pl.semaphore_wait(cred_out, 1)
 
             outward(k).start()
 
+        turned[k] = from_inner[k, 0].T
         for copy in stores(u):
             copy.start()
         acc[t, 0] += jnp.dot(from_inner[k, 0], dn_v[c], preferred_element_type=F32)
@@ -297,7 +300,7 @@
     def phase4(t):
         share_copy(t).wait()
 
-    phases = ((0, phase0), (2, phase1), (4, phase2), (6, phase3))
+    phases = ((0, phase0), (2, phase1), (5, phase2), (8, phase3))
     late = []
 
     @pl.loop(0, steps + lag)
@@ -325,69 +328,69 @@
     for u in range(steps - DEFER, steps):
         release(u)
 
-    @pl.loop(steps - SLOTS, steps)
+    @pl.loop(steps - slots, steps)
     def _(s):
-        inward(lax.rem(s, SLOTS), True).wait_send()
+        inward(lax.rem(s, slots), True).wait_send()
 
     for t in range(halves):
         phase4(t)
 
 
-def grads_kernel(block, x, ct, act, hg, keep_up, keep_dn, up_out, dn_out, xt):
+def grads_kernel(block, x, ct, act, hg, sums, keep_up, keep_dn, out, in_grad, up_out, dn_out, xt, sem):
     c = pl.program_id(0)
     width = hg.shape[1]
     per = width // block
+    d_model = ct.shape[1]
+    tall = 4 * block if d_model % (4 * block) == 0 else block
+    moves = [pltpu.make_async_copy(sums.at[i], ref, sem.at[i]) for i, ref in enumerate((out, in_grad))]
 
     @pl.when(c == 0)
     def _():
+        for move in moves:
+            move.start()
         xt[...] = x[...].T
 
-    @pl.loop(0, xt.shape[0] // block // 2)
-    def _(pair):
-        at = pl.ds(pl.multiple_of(pair * 2 * block, 2 * block), 2 * block)
-        full = jnp.dot(xt[at, :], hg[...], preferred_element_type=F32)
-        for i in range(2):
+    for top in range(0, d_model, tall):
+        full = jnp.dot(xt[top:top + tall, :], hg[...], preferred_element_type=F32)
+        for i in range(0, tall, block):
             for j in range(per):
                 lanes = slice(j * block, (j + 1) * block)
-                keep = keep_up[pair * 2 + i, c * per + j]
-                there = pl.ds(pl.multiple_of((pair * 2 + i) * block, block), block)
-                up_out[there, lanes] = (full[i * block:(i + 1) * block, lanes] * keep).astype(BF16)
-
-    at_t = act[...].T
-
-    @pl.loop(0, ct.shape[1] // block // 2)
-    def _(pair):
-        at = pl.ds(pl.multiple_of(pair * 2 * block, 2 * block), 2 * block)
-        full = jnp.dot(at_t, ct[:, at], preferred_element_type=F32)
-        for i in range(2):
-            there = pl.ds(pl.multiple_of((pair * 2 + i) * block, block), block)
-            for j in range(per):
-                lanes = slice(j * block, (j + 1) * block)
-                keep = keep_dn[c * per + j, pair * 2 + i]
-                dn_out[lanes, there] = (full[lanes, i * block:(i + 1) * block] * keep).astype(BF16)
+                keep = keep_up[(top + i) // block, c * per + j].astype(F32)
+                up_out[top + i:top + i + block, lanes] = (full[i:i + block, lanes] * keep).astype(BF16)
+        there = slice(top, top + tall)
+        full = jnp.dot(act[...], ct[:, there], preferred_element_type=F32)
+        for j in range(per):
+            lanes = slice(j * block, (j + 1) * block)
+            for i in range(0, tall, block):
+                keep = keep_dn[c * per + j, (top + i) // block].astype(F32)
+                dn_out[lanes, top + i:top + i + block] = (full[lanes, i:i + block] * keep).astype(BF16)
+
+    @pl.when(c == pl.num_programs(0) - 1)
+    def _():
+        for move in moves:
+            move.wait()
 
 
 def body(rows, cols, inputs, up_weight, down_weight, up_mask, down_mask, cotangent):
     tokens, d_model = inputs.shape
     hidden = up_weight.shape[1]
     block = d_model // up_mask.shape[0]
-    keep_up = (up_mask > 0).astype(F32)
-    keep_dn = (down_mask > 0).astype(F32)
     width = 2 * block if hidden % (2 * block) == 0 else block
     chunks = hidden // width
-    halves = 2
+    halves = next(h for h in (4, 2, 1) if tokens % (h * cols * 16) == 0)
     tm = tokens // halves
     chips = cols // 2
     part = tm // cols
+    slots = min(3 * halves, halves * chunks)
     vmem = pl.BlockSpec(memory_space=pltpu.VMEM)
     smem = pl.BlockSpec(memory_space=pltpu.SMEM)
     hbm = pl.BlockSpec(memory_space=pl.ANY)
     dma = pltpu.SemaphoreType.DMA
     sums, act, hg = pl.pallas_call(
-        functools.partial(layer_kernel, rows, cols, halves, width, block),
+        functools.partial(layer_kernel, rows, cols, halves, width, block, slots),
         out_shape=(
             jax.ShapeDtypeStruct((2, tokens, d_model), BF16),
-            jax.ShapeDtypeStruct((tokens, hidden), BF16),
+            jax.ShapeDtypeStruct((hidden, tokens), BF16),
             jax.ShapeDtypeStruct((tokens, hidden), BF16),
         ),
         in_specs=[vmem, vmem, hbm, hbm, smem, smem],
@@ -396,17 +399,18 @@
             pltpu.VMEM((chunks, d_model, width), BF16),
             pltpu.VMEM((chunks, width, d_model), BF16),
             pltpu.VMEM((halves, 2, tm, d_model), F32),
-            pltpu.VMEM((SLOTS, 2, tm, width), BF16),
-            pltpu.VMEM((SLOTS, 2, tm, width), BF16),
-            pltpu.VMEM((SLOTS, 2, tm, width), BF16),
+            pltpu.VMEM((slots, 2, tm, width), BF16),
+            pltpu.VMEM((slots, 2, tm, width), BF16),
+            pltpu.VMEM((slots, 2, tm, width), BF16),
+            pltpu.VMEM((slots, width, tm), BF16),
             pltpu.VMEM((halves, 2, tm // 2, d_model), BF16),
             pltpu.VMEM((halves, 2, tm // 2, d_model), BF16),
             pltpu.VMEM((halves, chips, 2, part, d_model), BF16),
             pltpu.VMEM((halves, max(chips - 1, 1), 2, part, d_model), BF16),
             pltpu.VMEM((halves, 2, part, d_model), BF16),
             dma((2, chunks)),
-            dma((SLOTS,)), dma((SLOTS,)), dma((SLOTS,)), dma((SLOTS,)),
-            dma((2, SLOTS)),
+            dma((slots,)), dma((slots,)), dma((slots,)), dma((slots,)),
+            dma((2, slots)),
             pltpu.SemaphoreType.REGULAR, pltpu.SemaphoreType.REGULAR,
             dma((halves,)), dma((halves,)),
             dma((halves, max(chips - 1, 1))), dma((halves, max(chips - 1, 1))),
@@ -417,33 +421,36 @@
         compiler_params=pltpu.CompilerParams(collective_id=0, has_side_effects=True, vmem_limit_bytes=LIMIT),
         cost_estimate=pl.CostEstimate(
             flops=8 * tokens * d_model * hidden, bytes_accessed=4 * d_model * hidden, transcendentals=tokens * hidden),
-    )(inputs, cotangent, up_weight, down_weight, keep_up, keep_dn)
+    )(inputs, cotangent, up_weight, down_weight, up_mask, down_mask)
 
     wide = next(w for w in (4 * block, 2 * block, block) if hidden % w == 0)
-    up_grad, down_grad = pl.pallas_call(
+    output, input_grad, up_grad, down_grad = pl.pallas_call(
         functools.partial(grads_kernel, block),
         grid=(hidden // wide,),
         out_shape=(
+            jax.ShapeDtypeStruct((tokens, d_model), BF16),
+            jax.ShapeDtypeStruct((tokens, d_model), BF16),
             jax.ShapeDtypeStruct((d_model, hidden), BF16),
             jax.ShapeDtypeStruct((hidden, d_model), BF16),
         ),
         in_specs=[
             pl.BlockSpec((tokens, d_model), lambda c: (0, 0)),
             pl.BlockSpec((tokens, d_model), lambda c: (0, 0)),
+            pl.BlockSpec((wide, tokens), lambda c: (c, 0)),
             pl.BlockSpec((tokens, wide), lambda c: (0, c)),
-            pl.BlockSpec((tokens, wide), lambda c: (0, c)),
-            smem, smem,
+            hbm, smem, smem,
         ],
         out_specs=(
+            hbm, hbm,
             pl.BlockSpec((d_model, wide), lambda c: (0, c)),
             pl.BlockSpec((wide, d_model), lambda c: (c, 0)),
         ),
-        scratch_shapes=[pltpu.VMEM((d_model, tokens), BF16)],
+        scratch_shapes=[pltpu.VMEM((d_model, tokens), BF16), dma((2,))],
         compiler_params=pltpu.CompilerParams(vmem_limit_bytes=48 * 1024 * 1024),
         cost_estimate=pl.CostEstimate(
             flops=4 * tokens * d_model * hidden, bytes_accessed=4 * d_model * hidden, transcendentals=0),
-    )(inputs, cotangent, act, hg, keep_up, keep_dn)
-    return (sums[0], sums[1], up_grad, down_grad)
+    )(inputs, cotangent, act, hg, sums, up_mask, down_mask)
+    return (output, input_grad, up_grad, down_grad)
 
 
 def solution(mesh):

time: 269 us -> 342 us (1.27)
  Pallas kernels: 260 us -> 337 us
    pallas_call x1, Pallas kernels: 41.7 us -> 131 us  [body(): pl.pallas_call(functools.partial(grads_kernel, block), grid=(hidden // wi...]
    pallas_call x1, Pallas kernels: 218 us -> 206 us  [body(): pl.pallas_call(functools.partial(layer_kernel, rows, cols, halves, width,...]
    squeeze x1 -> x0, local copies, waits for them, and re-layouts: 4.97 us -> none  [body(): return (sums[0], sums[1], up_grad, down_grad)]
    unnamed x9, local copies, waits for them, and re-layouts: 0.81 us -> 4.57 us
where the time goes in v2:
time: 342 us
  Pallas kernels  337 us (99%)
  local copies, waits for them, and re-layouts  4.57 us (1%)
    pallas_call x1, Pallas kernels, body(): pl.pallas_call(functools.partial(layer_kernel, rows, cols, halves, width,...  206 us
    pallas_call x1, Pallas kernels, body(): pl.pallas_call(functools.partial(grads_kernel, block), grid=(hidden // wi...  131 us

profile of v2, /device:TPU:0, one launch (start us, length us, event | category | flops | bytes accessed | tf_op | source)
XLA Modules:
  0.0 342.2 jit_solution(13039705665302657132)
XLA Ops:
  0.6 1.4 copy.10.keep_dn
  2.0 0.0 copy-start
  2.0 0.0 copy-start.3
  2.0 205.6 %shard_map.93 = (bf16[2,512,2048]{2,1,0:T(8,128)(2,1)}, bf16[3584,512]{1,0:T(8,128)(2,1)}, bf16[512,3584]{1,0:T(8,128)(2,1)}) custom-call(bf16[512,2048]{1,0:T(8,128)(2,1)} %x.3, bf16[512,2048]{1,0:T(8,128)(2,1)} %ct.3, bf16[2048,3584]{1,0:T(8,128)(2,1)} %up_hbm.1, bf16[3584,2048]{1,0:T(8,128)(2,1)} %dn_hbm.1, s32[16,28]{1,0:T(8,128)} %keep_up.3, ...), custom_call_target="tpu_custom_call" | custom-call | flops 30064771072 | bytes 29360128 | tf_op jit(solution)/shard_map/pallas_call | solution.py:389
  207.6 0.0 copy-done
  207.6 0.0 copy-done.3
  207.6 0.0 copy-start.1
  207.7 1.6 copy-done.1
  209.2 0.0 copy-start.2
  209.2 1.6 copy-done.2
  210.8 131.4 %shard_map.94 = (bf16[512,2048]{1,0:T(8,128)(2,1)}, bf16[512,2048]{1,0:T(8,128)(2,1)}, bf16[2048,3584]{1,0:T(8,128)(2,1)}, bf16[3584,2048]{1,0:T(8,128)(2,1)}) custom-call(bf16[512,2048]{1,0:T(8,128)(2,1)S(1)} %copy-done.1, bf16[512,2048]{1,0:T(8,128)(2,1)S(1)} %copy-done.2, bf16[3584,512]{1,0:T(8,128)(2,1)} %get-tuple-element.7.act, ...), custom_call_target="tpu_custom_call" | custom-call | flops 15032385536 | bytes 29360128 | tf_op jit(solution)/shard_map/pallas_call | solution.py:427
Async XLA Ops:
  2.0 205.6 %copy-start = (s32[28,16]{1,0:T(8,128)S(1)}, s32[28,16]{1,0:T(8,128)}, u32[]{:S(2)}) copy-start(s32[28,16]{1,0:T(8,128)} %copy.10.keep_dn) | copy-start | bytes 5380
  2.0 205.6 %copy-start.3 = (s32[16,28]{1,0:T(8,128)S(1)}, s32[16,28]{1,0:T(8,128)}, u32[]{:S(2)}) copy-start(s32[16,28]{1,0:T(8,128)} %keep_up.3) | copy-start | bytes 5380
  207.6 1.6 copy-start.1
  209.2 1.6 copy-start.2

commit v3 on v2

--- a/solution.py
+++ b/solution.py
@@ -36,7 +36,7 @@
     x, ct, up_hbm, dn_hbm, keep_up, keep_dn,
     sums, act_hbm, hg_hbm,
     up_v, dn_v, acc, to_inner, from_outer, from_inner, turned,
-    pair_out, pair_in, half, chip_in, fin,
+    pair_out, pair_in, half, chip_in, share_in,
     w_sem, in_send, out_recv, in_recv, out_send, store_sem, cred_in, cred_out,
     s0, r0, s1, r1, s2, r2, s3, r3, own_sem,
 ):
@@ -243,22 +243,24 @@
             send_sem=s1.at[t, j - 1], recv_sem=r1.at[t, j - 1],
             device_id=chip_peer(j), device_id_type=MESH)
 
+    mine = pl.ds(pl.multiple_of(chip * part, part), part)
+
     def spread_copy(t, j):
-        mine = rows_of(t, core, chip * part, part)
-        return pltpu.make_async_remote_copy(
-            src_ref=fin.at[t], dst_ref=sums.at[:, mine, :],
-            send_sem=s2.at[t, j - 1], recv_sem=r2.at[t, j - 1],
+        place = pair_out.at[t, :, mine, :]
+        return pltpu.make_async_remote_copy(
+            src_ref=place, dst_ref=place, send_sem=s2.at[t, j - 1], recv_sem=r2.at[t, j - 1],
             device_id=chip_peer(j), device_id_type=MESH)
 
-    def own_copy(t):
-        mine = rows_of(t, core, chip * part, part)
-        return pltpu.make_async_copy(fin.at[t], sums.at[:, mine, :], own_sem.at[t])
-
     def share_copy(t):
-        mine = rows_of(t, core, 0, tm // 2)
-        return pltpu.make_async_remote_copy(
-            src_ref=sums.at[:, mine, :], dst_ref=sums.at[:, mine, :], send_sem=s3.at[t], recv_sem=r3.at[t],
+        return pltpu.make_async_remote_copy(
+            src_ref=pair_out.at[t], dst_ref=share_in.at[t], send_sem=s3.at[t], recv_sem=r3.at[t],
             device_id=sibling, device_id_type=MESH)
+
+    def own_store(t):
+        return pltpu.make_async_copy(pair_out.at[t], sums.at[:, rows_of(t, core, 0, tm // 2), :], own_sem.at[t, 0])
+
+    def share_store(t):
+        return pltpu.make_async_copy(share_in.at[t], sums.at[:, rows_of(t, 1 - core, 0, tm // 2), :], own_sem.at[t, 1])
 
     def phase0(t):
         other = pl.ds(pl.multiple_of((1 - core) * (tm // 2), tm // 2), tm // 2)
@@ -271,10 +273,10 @@
 
         @pl.loop(0, chips)
         def _(q):
-            mine = pl.ds(pl.multiple_of(core * (tm // 2) + q * part, part), part)
+            held = pl.ds(pl.multiple_of(core * (tm // 2) + q * part, part), part)
             there = pl.ds(pl.multiple_of(q * part, part), part)
             for which in range(2):
-                half[t, q, which] = (acc[t, which, mine, :] + pair_in[t, which, there, :].astype(F32)).astype(BF16)
+                half[t, q, which] = (acc[t, which, held, :] + pair_in[t, which, there, :].astype(F32)).astype(BF16)
 
         for j in range(1, chips):
             chip_copy(t, j).start()
@@ -286,19 +288,21 @@
             total = half[t, chip, which].astype(F32)
             for j in range(1, chips):
                 total = total + chip_in[t, j - 1, which].astype(F32)
-            fin[t, which] = total.astype(BF16)
-        own_copy(t).start()
+            pair_out[t, which, mine, :] = total.astype(BF16)
         for j in range(1, chips):
             spread_copy(t, j).start()
 
     def phase3(t):
-        own_copy(t).wait()
         for j in range(1, chips):
             spread_copy(t, j).wait()
         share_copy(t).start()
+        own_store(t).start()
 
     def phase4(t):
         share_copy(t).wait()
+        share_store(t).start()
+        own_store(t).wait()
+        share_store(t).wait()
 
     phases = ((0, phase0), (2, phase1), (5, phase2), (8, phase3))
     late = []
@@ -336,39 +340,34 @@
         phase4(t)
 
 
-def grads_kernel(block, x, ct, act, hg, sums, keep_up, keep_dn, out, in_grad, up_out, dn_out, xt, sem):
+def grads_kernel(block, x, ct, act, hg, sums, keep_up, keep_dn, out, in_grad, up_out, dn_out, xt):
     c = pl.program_id(0)
     width = hg.shape[1]
     per = width // block
     d_model = ct.shape[1]
-    tall = 4 * block if d_model % (4 * block) == 0 else block
-    moves = [pltpu.make_async_copy(sums.at[i], ref, sem.at[i]) for i, ref in enumerate((out, in_grad))]
+    tall = next(b for b in (4 * block, 2 * block, block) if d_model % b == 0)
+    out[...] = sums[0]
+    in_grad[...] = sums[1]
 
     @pl.when(c == 0)
     def _():
-        for move in moves:
-            move.start()
         xt[...] = x[...].T
 
-    for top in range(0, d_model, tall):
-        full = jnp.dot(xt[top:top + tall, :], hg[...], preferred_element_type=F32)
+    @pl.loop(0, d_model // tall)
+    def _(b):
+        top = pl.multiple_of(b * tall, tall)
+        there = pl.ds(top, tall)
+        up = jnp.dot(xt[there, :], hg[...], preferred_element_type=F32)
+        dn = jnp.dot(act[...], ct[:, there], preferred_element_type=F32)
         for i in range(0, tall, block):
+            place = pl.ds(pl.multiple_of(top + i, block), block)
+            which = b * (tall // block) + i // block
             for j in range(per):
                 lanes = slice(j * block, (j + 1) * block)
-                keep = keep_up[(top + i) // block, c * per + j].astype(F32)
-                up_out[top + i:top + i + block, lanes] = (full[i:i + block, lanes] * keep).astype(BF16)
-        there = slice(top, top + tall)
-        full = jnp.dot(act[...], ct[:, there], preferred_element_type=F32)
-        for j in range(per):
-            lanes = slice(j * block, (j + 1) * block)
-            for i in range(0, tall, block):
-                keep = keep_dn[c * per + j, (top + i) // block].astype(F32)
-                dn_out[lanes, top + i:top + i + block] = (full[lanes, i:i + block] * keep).astype(BF16)
-
-    @pl.when(c == pl.num_programs(0) - 1)
-    def _():
-        for move in moves:
-            move.wait()
+                keep = keep_up[which, c * per + j].astype(F32)
+                up_out[place, lanes] = (up[i:i + block, lanes] * keep).astype(BF16)
+                keep = keep_dn[c * per + j, which].astype(F32)
+                dn_out[lanes, place] = (dn[lanes, i:i + block] * keep).astype(BF16)
 
 
 def body(rows, cols, inputs, up_weight, down_weight, up_mask, down_mask, cotangent):
@@ -407,7 +406,7 @@
             pltpu.VMEM((halves, 2, tm // 2, d_model), BF16),
             pltpu.VMEM((halves, chips, 2, part, d_model), BF16),
             pltpu.VMEM((halves, max(chips - 1, 1), 2, part, d_model), BF16),
-            pltpu.VMEM((halves, 2, part, d_model), BF16),
+            pltpu.VMEM((halves, 2, tm // 2, d_model), BF16),
             dma((2, chunks)),
             dma((slots,)), dma((slots,)), dma((slots,)), dma((slots,)),
             dma((2, slots)),
@@ -416,7 +415,7 @@
             dma((halves, max(chips - 1, 1))), dma((halves, max(chips - 1, 1))),
             dma((halves, max(chips - 1, 1))), dma((halves, max(chips - 1, 1))),
             dma((halves,)), dma((halves,)),
-            dma((halves,)),
+            dma((halves, 2)),
         ],
         compiler_params=pltpu.CompilerParams(collective_id=0, has_side_effects=True, vmem_limit_bytes=LIMIT),
         cost_estimate=pl.CostEstimate(
@@ -424,6 +423,7 @@
     )(inputs, cotangent, up_weight, down_weight, up_mask, down_mask)
 
     wide = next(w for w in (4 * block, 2 * block, block) if hidden % w == 0)
+    pieces = next(n for n in (4, 2, 1) if n <= hidden // wide and tokens % (n * 16) == 0)
     output, input_grad, up_grad, down_grad = pl.pallas_call(
         functools.partial(grads_kernel, block),
         grid=(hidden // wide,),
@@ -438,15 +438,17 @@
             pl.BlockSpec((tokens, d_model), lambda c: (0, 0)),
             pl.BlockSpec((wide, tokens), lambda c: (c, 0)),
             pl.BlockSpec((tokens, wide), lambda c: (0, c)),
-            hbm, smem, smem,
+            pl.BlockSpec((2, tokens // pieces, d_model), lambda c: (0, jnp.minimum(c, pieces - 1), 0)),
+            smem, smem,
         ],
         out_specs=(
-            hbm, hbm,
+            pl.BlockSpec((tokens // pieces, d_model), lambda c: (jnp.minimum(c, pieces - 1), 0)),
+            pl.BlockSpec((tokens // pieces, d_model), lambda c: (jnp.minimum(c, pieces - 1), 0)),
             pl.BlockSpec((d_model, wide), lambda c: (0, c)),
             pl.BlockSpec((wide, d_model), lambda c: (c, 0)),
         ),
-        scratch_shapes=[pltpu.VMEM((d_model, tokens), BF16), dma((2,))],
-        compiler_params=pltpu.CompilerParams(vmem_limit_bytes=48 * 1024 * 1024),
+        scratch_shapes=[pltpu.VMEM((d_model, tokens), BF16)],
+        compiler_params=pltpu.CompilerParams(vmem_limit_bytes=LIMIT),
         cost_estimate=pl.CostEstimate(
             flops=4 * tokens * d_model * hidden, bytes_accessed=4 * d_model * hidden, transcendentals=0),
     )(inputs, cotangent, act, hg, sums, up_mask, down_mask)

time: 342 us -> 239 us (0.70)
  Pallas kernels: 337 us -> 237 us
    pallas_call x1, Pallas kernels: 131 us -> 29.7 us  [body(): pl.pallas_call(functools.partial(grads_kernel, block), grid=(hidden // wi...]
where the time goes in v3:
time: 239 us
  Pallas kernels  237 us (99%)
    pallas_call x1, Pallas kernels, body(): pl.pallas_call(functools.partial(layer_kernel, rows, cols, halves, width,...  207 us
    pallas_call x1, Pallas kernels, body(): pl.pallas_call(functools.partial(grads_kernel, block), grid=(hidden // wi...  29.7 us

profile of v3, /device:TPU:0, one launch (start us, length us, event | category | flops | bytes accessed | tf_op | source)
XLA Modules:
  0.0 239.0 jit_solution(12115795489514759253)
XLA Ops:
  0.6 1.4 copy.10.keep_dn
  2.0 207.2 %shard_map.93 = (bf16[2,512,2048]{2,1,0:T(8,128)(2,1)}, bf16[3584,512]{1,0:T(8,128)(2,1)}, bf16[512,3584]{1,0:T(8,128)(2,1)}) custom-call(bf16[512,2048]{1,0:T(8,128)(2,1)} %x.3, bf16[512,2048]{1,0:T(8,128)(2,1)} %ct.3, bf16[2048,3584]{1,0:T(8,128)(2,1)} %up_hbm.1, bf16[3584,2048]{1,0:T(8,128)(2,1)} %dn_hbm.1, s32[16,28]{1,0:T(8,128)} %keep_up.3, ...), custom_call_target="tpu_custom_call" | custom-call | flops 30064771072 | bytes 29360128 | tf_op jit(solution)/shard_map/pallas_call | solution.py:388
  209.2 29.7 %shard_map.94 = (bf16[512,2048]{1,0:T(8,128)(2,1)}, bf16[512,2048]{1,0:T(8,128)(2,1)}, bf16[2048,3584]{1,0:T(8,128)(2,1)}, bf16[3584,2048]{1,0:T(8,128)(2,1)}) custom-call(bf16[512,2048]{1,0:T(8,128)(2,1)} %x.3, bf16[512,2048]{1,0:T(8,128)(2,1)} %ct.3, bf16[3584,512]{1,0:T(8,128)(2,1)} %get-tuple-element.7.act, bf16[512,3584]{1,0:T(8,128)(2,1)} %get-tuple-element.8.hg, ...), custom_call_target="tpu_custom_call" | custom-call | flops 15032385536 | bytes 29360128 | tf_op jit(solution)/shard_map/pallas_call | solution.py:427

commit v4 on v3

--- a/solution.py
+++ b/solution.py
@@ -353,7 +353,7 @@
     def _():
         xt[...] = x[...].T
 
-    @pl.loop(0, d_model // tall)
+    @pl.loop(0, d_model // tall, unroll=2 if d_model // tall % 2 == 0 else 1)
     def _(b):
         top = pl.multiple_of(b * tall, tall)
         there = pl.ds(top, tall)

time: 239 us -> 237 us (level)
  no operation moved by 1% of the time
where the time goes in v4:
time: 237 us
  Pallas kernels  235 us (99%)
    pallas_call x1, Pallas kernels, body(): pl.pallas_call(functools.partial(layer_kernel, rows, cols, halves, width,...  207 us
    pallas_call x1, Pallas kernels, body(): pl.pallas_call(functools.partial(grads_kernel, block), grid=(hidden // wi...  27.5 us

profile of v4, /device:TPU:0, one launch (start us, length us, event | category | flops | bytes accessed | tf_op | source)
XLA Modules:
  0.0 236.8 jit_solution(10275553931346150777)
XLA Ops:
  0.6 1.4 copy.10.keep_dn
  2.0 207.2 %shard_map.93 = (bf16[2,512,2048]{2,1,0:T(8,128)(2,1)}, bf16[3584,512]{1,0:T(8,128)(2,1)}, bf16[512,3584]{1,0:T(8,128)(2,1)}) custom-call(bf16[512,2048]{1,0:T(8,128)(2,1)} %x.3, bf16[512,2048]{1,0:T(8,128)(2,1)} %ct.3, bf16[2048,3584]{1,0:T(8,128)(2,1)} %up_hbm.1, bf16[3584,2048]{1,0:T(8,128)(2,1)} %dn_hbm.1, s32[16,28]{1,0:T(8,128)} %keep_up.3, ...), custom_call_target="tpu_custom_call" | custom-call | flops 30064771072 | bytes 29360128 | tf_op jit(solution)/shard_map/pallas_call | solution.py:388
  209.2 27.5 %shard_map.94 = (bf16[512,2048]{1,0:T(8,128)(2,1)}, bf16[512,2048]{1,0:T(8,128)(2,1)}, bf16[2048,3584]{1,0:T(8,128)(2,1)}, bf16[3584,2048]{1,0:T(8,128)(2,1)}) custom-call(bf16[512,2048]{1,0:T(8,128)(2,1)} %x.3, bf16[512,2048]{1,0:T(8,128)(2,1)} %ct.3, bf16[3584,512]{1,0:T(8,128)(2,1)} %get-tuple-element.7.act, bf16[512,3584]{1,0:T(8,128)(2,1)} %get-tuple-element.8.hg, ...), custom_call_target="tpu_custom_call" | custom-call | flops 15032385536 | bytes 29360128 | tf_op jit(solution)/shard_map/pallas_call | solution.py:427
